TPU v7x, 512 devices: a whole 4x8x8 slice. The times are simulated.
512 devices in a mesh: perm: 16 (over y, core), summa: 32 (over z, x).
Axes of the slice: x: 4, y: 8, z: 8, core: 2. Of those that a mesh axis runs over, the one named last changes fastest.
Arguments:
- amplitudes: bfloat16 [16, 1024, 1024], P('perm', None, 'summa'), may hold values from -6 to 6
- cycle_panels: bfloat16 [16, 128, 64, 1024], P('perm', None, 'summa'), may hold values from -0.75 to 0.75
- tile_mask: int32 [8, 2, 8, 8], replicated, may hold values 0 or 1
- panel_slot: int32 [16], replicated, may hold values from 0 to 15, each once
- window_blocks: int32 [4], replicated, may hold values from 0 to 7, as said below
- virt_energy: float32 [1024], replicated, may hold values from 0.5 to 3
- row_energy: float32 [8], replicated, may hold values from -2 to -0.5
- col_energy: float32 [64], P('summa'), may hold values from -2 to -0.5
Outputs:
- update: bfloat16 [1024, 8, 64, 1024], P('perm', None, 'summa')
Inputs may be any that keep to these rules, and one draw needn't show every extreme that they name: `panel_slot`: a permutation: each of the 16 slots holds exactly one panel. `window_blocks`: 4 distinct tile numbers in no particular order; tile 0 and tile 8 - 1 are always among them.
All inputs are finite; a program needn't handle non-finite values.
Results may differ from a plain program's by a relative error of at most 0.001.
Values may be sent and summed in bfloat16 or wider, within the bound.
No kernel may reach another device: no remote copies, remote signals or barrier semaphores. Data moves between devices by JAX's collectives and lax.ppermute only.
A program may use at most 64 MiB of HBM per device.

v0:
```python
import jax
import jax.numpy as jnp
from jax import lax
from jax.experimental import pallas as pl
from jax.experimental.pallas import tpu as pltpu
from jax.sharding import PartitionSpec as P

CORES, CHIPS_Z, CHIPS_X = 2, 8, 4
ORDER_Z, ORDER_X = (7, 3, 6, 2, 5, 1, 4, 0), (3, 1, 2, 0)
ALONG_Z = [[z * CHIPS_X + x for z in ORDER_Z] for x in range(CHIPS_X)]
ALONG_X = [[z * CHIPS_X + x for x in ORDER_X] for z in range(CHIPS_Z)]
MIB = 1024 * 1024
LANES, MXU = 128, 256


def gather_by_exchange(value, groups):
    count = len(groups[0])
    copies = jnp.broadcast_to(value[None], (count, *value.shape))
    return lax.all_to_all(copies, "summa", 0, 0, axis_index_groups=groups, tiled=True)


def together(parts, cols, some):
    count = parts * cols * some
    to = lax.broadcasted_iota(jnp.int32, (count, count), 0)
    of = lax.broadcasted_iota(jnp.int32, (count, count), 1)
    here = of == to % (parts * cols) * some + to // (parts * cols)
    return here.astype(jnp.float32).astype(jnp.bfloat16)


def rows_kernel(keep, tiles, out, rows):
    x_count, windows, occ_rows, c_local, lanes = tiles.shape
    half, width = rows.shape[0], x_count * c_local
    summed = lanes // half
    for i in range(occ_rows):
        for w in range(windows):
            tile = jnp.concatenate([tiles[ORDER_X.index(x), w, i] for x in range(x_count)], axis=0)
            tile = tile.astype(jnp.float32).T
            for k in range(summed):
                rows[:, i, pl.ds((k * windows + w) * width, width)] = (
                    tile[k * half : (k + 1) * half] * keep[k * windows + w, pl.ds(i, 1), :]
                )
    out[...] = rows[...].reshape(out.shape).astype(out.dtype)


def amplitude_rows(keep, tiles):
    x_count, windows, occ_rows, c_local, lanes = tiles.shape
    summed = keep.shape[0] // windows
    half, depth = lanes // summed, summed * windows * x_count * c_local
    vmem = pl.BlockSpec(memory_space=pltpu.VMEM)
    return pl.pallas_call(
        rows_kernel,
        out_shape=jax.ShapeDtypeStruct((half * occ_rows, depth), jnp.bfloat16),
        in_specs=[vmem, vmem],
        out_specs=vmem,
        scratch_shapes=[pltpu.VMEM((half, occ_rows, depth), jnp.float32)],
        compiler_params=pltpu.CompilerParams(vmem_limit_bytes=16 * MIB),
    )(keep, tiles)


def contract_kernel(
    chosen, lhs, row_energy, col_energy, slots, out, panels, values, done, came, left
):
    row_count, depth = lhs.shape
    cols, count, _, _ = panels.shape
    width = depth // count
    parts = panels.shape[2] // width
    fetches = []
    slot = [jnp.max(chosen[pl.ds(m, 1), :]) for m in range(count)]
    for j in range(cols):
        for m in range(count):
            rows = pl.ds(j * parts * width, parts * width)
            fetches.append(
                pltpu.make_async_copy(slots.at[slot[m], rows], panels.at[j, m], came.at[j, m])
            )
    for fetch in fetches:
        fetch.start()
    beside = MXU // LANES
    some = MXU // (parts * cols)
    order = together(parts, cols, some)
    steps = [(j, part) for j in range(cols) for part in range(0, parts, beside)]

    def product(j, part):
        if part == 0:
            for fetch in fetches[j * count : (j + 1) * count]:
                fetch.wait()
        rhs = [
            panels[j, :, pl.ds(one * width, width), :].reshape(depth, LANES)
            for one in range(part, part + beside)
        ]
        return jnp.dot(
            lhs[...], jnp.concatenate(rhs, axis=1), preferred_element_type=jnp.float32
        )

    def finish(term, j, part):
        for one in range(beside):
            gap = row_energy[...] + col_energy[pl.ds(j, 1), pl.ds((part + one) * LANES, LANES)]
            guess = pl.reciprocal(gap, approx=True)
            value = term[:, one * LANES : (one + 1) * LANES] * (guess * (2.0 - gap * guess))
            values[part + one, j] = value.astype(out.dtype)

    term = product(*steps[0])
    for now, later in zip(steps, steps[1:] + [None]):
        ahead = product(*later) if later else None
        finish(term, *now)
        term = ahead
    stores = []
    rows_of = parts * cols
    span = row_count // left.shape[0]
    for m in range(0, row_count, some * beside):
        apart = [
            jnp.concatenate(
                [
                    values[part, j, pl.ds(m + one * some, some), :]
                    for part in range(parts)
                    for j in range(cols)
                ],
                axis=0,
            )
            for one in range(beside)
        ]
        mixed = jnp.dot(order, jnp.concatenate(apart, axis=1), preferred_element_type=jnp.float32)
        mixed = mixed.astype(out.dtype)
        for one in range(beside):
            done[pl.ds((m + one * some) * rows_of, MXU), :] = mixed[:, one * LANES : (one + 1) * LANES]
        if (m + some * beside) % span == 0:
            rows = pl.ds((m + some * beside - span) * rows_of, span * rows_of)
            store = pltpu.make_async_copy(done.at[rows], out.at[rows], left.at[m // span])
            store.start()
            stores.append(store)
    for store in stores:
        store.wait()


def contract(chosen, lhs, row_energy, col_energy, slots):
    row_count, depth = lhs.shape
    cols, width_virt = col_energy.shape
    parts = width_virt // LANES
    width = slots.shape[1] // (parts * cols)
    count = depth // width
    vmem = pl.BlockSpec(memory_space=pltpu.VMEM)
    hbm = pl.BlockSpec(memory_space=pltpu.HBM)
    return pl.pallas_call(
        contract_kernel,
        out_shape=jax.ShapeDtypeStruct((row_count * parts * cols, LANES), jnp.bfloat16),
        in_specs=[vmem] * 4 + [hbm],
        out_specs=hbm,
        scratch_shapes=[
            pltpu.VMEM((cols, count, parts * width, LANES), slots.dtype),
            pltpu.VMEM((parts, cols, row_count, LANES), jnp.bfloat16),
            pltpu.VMEM((row_count * parts * cols, LANES), jnp.bfloat16),
            pltpu.SemaphoreType.DMA((cols, count)),
            pltpu.SemaphoreType.DMA((8,)),
        ],
        compiler_params=pltpu.CompilerParams(vmem_limit_bytes=24 * MIB),
    )(
        chosen,
        lhs,
        row_energy,
        col_energy,
        pltpu.with_memory_space_constraint(slots, pltpu.HBM),
    )


def body(
    amplitudes,
    cycle_panels,
    tile_mask,
    panel_slot,
    window_blocks,
    virt_energy,
    row_energy,
    col_energy,
):
    _, _, col_local, width_virt = cycle_panels.shape
    c_local = amplitudes.shape[2]
    occ_rows, occ_summed = tile_mask.shape[:2]
    perm_count = lax.axis_size("perm")
    a_local = amplitudes.shape[1] // perm_count
    p = lax.axis_index("perm")

    width, parts = cycle_panels.shape[1], width_virt // LANES
    as_given = jnp.swapaxes(cycle_panels.reshape(width, col_local, parts, LANES), 1, 2)
    as_given = lax.optimization_barrier(as_given.reshape(-1, LANES))
    by_part = jnp.transpose(as_given.reshape(width, parts, col_local, LANES), (2, 1, 0, 3))
    slots = lax.all_gather(by_part.reshape(-1, LANES), "perm", axis=0)

    blocks = jnp.swapaxes(amplitudes[0].T.reshape(c_local, perm_count, a_local), 0, 1)
    blocks = lax.all_to_all(blocks, "perm", 0, 0, tiled=True)
    blocks, virt_energy, row_energy = lax.optimization_barrier((blocks, virt_energy, row_energy))
    blocks = blocks.reshape(occ_rows, occ_summed, c_local, a_local)
    blocks = jnp.concatenate([blocks[:, k] for k in range(occ_summed)], axis=-1)
    row_virt = lax.dynamic_slice_in_dim(virt_energy, p * a_local, a_local)
    rows = row_virt[:, None] - row_energy[None, :]
    rows = jnp.broadcast_to(rows[..., None], (*rows.shape, LANES)).reshape(-1, LANES)
    columns = virt_energy[None, :] - col_energy[:, None]
    tiles = gather_by_exchange(blocks, ALONG_Z)
    place = CHIPS_Z - 1 - window_blocks
    place = (place << 1 | place >> 2) & (CHIPS_Z - 1)
    tiles = jnp.stack(
        [lax.dynamic_index_in_dim(tiles, place[w], 0, False) for w in range(place.shape[0])]
    )
    tiles, tile_mask, panel_slot, window_blocks = lax.optimization_barrier(
        (tiles, tile_mask, panel_slot, window_blocks)
    )
    tiles = gather_by_exchange(tiles, ALONG_X)
    keep = lax.dynamic_index_in_dim(tile_mask, p // CORES, axis=2, keepdims=False)
    keep = jnp.take(keep, window_blocks, axis=2).transpose(1, 2, 0).reshape(-1, occ_rows)
    keep = jnp.broadcast_to(keep[..., None].astype(jnp.float32), (*keep.shape, LANES))
    chosen = jnp.take(panel_slot.reshape(occ_summed, -1), window_blocks, axis=1).reshape(-1)
    chosen = jnp.broadcast_to(chosen[:, None], (chosen.shape[0], LANES))
    tiles, rows, columns, keep, chosen = lax.optimization_barrier(
        (tiles, rows, columns, keep, chosen)
    )
    lhs = amplitude_rows(keep, tiles)
    result = contract(chosen, lhs, rows, columns, slots)
    result = jnp.swapaxes(result.reshape(-1, parts, col_local, LANES), 1, 2)
    return result.reshape(a_local, occ_rows, col_local, width_virt)


def solution(mesh):
    in_specs = (
        P("perm", None, "summa"),
        P("perm", None, "summa", None),
        P(),
        P(),
        P(),
        P(),
        P(),
        P("summa"),
    )
    out_specs = P("perm", None, "summa", None)
    return jax.shard_map(body, mesh=mesh, in_specs=in_specs, out_specs=out_specs, check_vma=False)
```

profile of v0, /device:TPU:1, one launch (start us, length us, event | category | flops | bytes accessed | tf_op | source)
XLA Modules:
  0.0 86.4 jit_solution(2989827681134420221)
XLA Ops:
  6.5 2.0 %copy.42 = bf16[2,8,128,128]{3,2,1,0:T(8,128)(2,1)} copy(bf16[2,8,128,128]{3,0,1,2:T(2,128)(2,1)} %bitcast.39) | data formatting | bytes 1048576 | tf_op jit(solution)/shard_map/transpose | solution.py:184
  8.6 1.0 %reshape.80 = bf16[32,16,64]{2,1,0:T(8,128)(2,1)S(1)} reshape(bf16[32,1024]{1,0:T(8,128)(2,1)} %bitcast.42) | data formatting | bytes 131072 | tf_op jit(solution)/shard_map/reshape | solution.py:187
  9.7 0.1 reshape.106
  9.8 17.1 %all_to_all.15 = bf16[16,2,1024]{2,1,0:T(2,128)(2,1)S(1)} all-to-all(bf16[16,2,1024]{2,1,0:T(2,128)(2,1)S(1)} %reshape.106), channel_id=1, replica_groups=mesh['perm'=16,'summa'=32] {'perm'}, dimensions={0} | all-to-all | bytes 131072 | tf_op jit(solution)/shard_map/all_to_all | solution.py:188
  26.9 0.1 reshape.107
  27.1 0.1 pad_maximum_fusion.1
  27.2 0.9 %broadcast_in_dim.26 = bf16[8,8,32,128]{3,2,1,0:T(8,128)(2,1)} broadcast(bf16[8,32,128]{2,1,0:T(8,128)(2,1)S(1)} %pad_maximum_fusion.1), dimensions={1,2,3} | broadcast | bytes 589824 | tf_op jit(solution)/shard_map/broadcast_in_dim | solution.py:18
  28.0 11.3 %all-to-all-start.1 = ((bf16[8,8,32,128]{3,2,1,0:T(8,128)(2,1)}), bf16[8,8,32,128]{3,2,1,0:T(8,128)(2,1)S(1)}, u32[]{:S(2)}, u32[]{:S(2)}) async-start(bf16[8,8,32,128]{3,2,1,0:T(8,128)(2,1)} %broadcast_in_dim.26), calls=%async_computation.1 | async-start | bytes 1048576 | tf_op jit(solution)/shard_map/all_to_all | solution.py:19
  39.4 0.7 or_and_fusion
  40.0 0.6 fusion
  47.7 0.8 dynamic_slice.24
  48.4 0.1 sub.42
  48.5 0.1 sub.43
  48.6 0.7 sub.44
  49.3 0.1 sub.45
  49.4 0.8 broadcast_subtract_fusion.col_energy
  50.1 0.7 all-to-all-done.1
  50.9 1.2 %broadcast_in_dim.29 = bf16[4,4,8,32,128]{4,3,2,1,0:T(8,128)(2,1)} broadcast(bf16[4,8,32,128]{3,2,1,0:T(8,128)(2,1)S(1)} %pad_maximum_fusion), dimensions={1,2,3,4} | broadcast | bytes 1310720 | tf_op jit(solution)/shard_map/broadcast_in_dim | solution.py:18
  52.1 6.0 %all-to-all-start.2 = ((bf16[4,4,8,32,128]{4,3,2,1,0:T(8,128)(2,1)}), bf16[4,4,8,32,128]{4,3,2,1,0:T(8,128)(2,1)S(1)}, u32[]{:S(2)}, u32[]{:S(2)}) async-start(bf16[4,4,8,32,128]{4,3,2,1,0:T(8,128)(2,1)} %broadcast_in_dim.29), calls=%async_computation.2 | async-start | bytes 2097152 | tf_op jit(solution)/shard_map/all_to_all | solution.py:19
  58.1 0.1 reshape.82
  58.1 0.1 copy.39
  58.2 0.6 gather_fusion.1
  58.9 0.1 copy.40
  59.0 0.1 select_n.59
  59.1 0.1 copy.37
  59.2 0.6 gather_fusion
  59.7 0.1 convert_bitcast_fusion
  59.8 9.7 %all-to-all-done.2.tiles = bf16[4,4,8,32,128]{4,3,2,1,0:T(8,128)(2,1)S(1)} async-done(((bf16[4,4,8,32,128]{4,3,2,1,0:T(8,128)(2,1)}), bf16[4,4,8,32,128]{4,3,2,1,0:T(8,128)(2,1)S(1)}, u32[]{:S(2)}, u32[]{:S(2)}) %all-to-all-start.2) | async-done | bytes 1048608 | tf_op jit(solution)/shard_map/all_to_all | solution.py:19
  69.5 0.1 broadcast_in_dim.30.row_energy
  69.8 1.5 %shard_map.82.lhs = bf16[512,1024]{1,0:T(8,128)(2,1)S(1)} custom-call(f32[8,8,128]{2,1,0:T(8,128)S(1)} %broadcast_in_dim.56.keep, bf16[4,4,8,32,128]{4,3,2,1,0:T(8,128)(2,1)S(1)} %all-to-all-done.2.tiles), custom_call_target="tpu_custom_call" | custom-call | tf_op jit(solution)/shard_map/pallas_call | solution.py:50
  71.3 2.3 %all-gather.2.cloned.1.call-done.slots = bf16[16,2048,128]{2,1,0:T(8,128)(2,1)} async-done(((bf16[1,2048,128]{2,1,0:T(8,128)(2,1)}), bf16[16,2048,128]{2,1,0:T(8,128)(2,1)}) %all-gather.2.cloned.1.call-update) | async-done | bytes 8388624 | tf_op jit(solution)/shard_map/all_gather | solution.py:185
  73.6 5.9 %shard_map.83 = bf16[8192,128]{1,0:T(8,128)(2,1)} custom-call(s32[8,128]{1,0:T(8,128)S(1)} %broadcast_in_dim.58.chosen, bf16[512,1024]{1,0:T(8,128)(2,1)S(1)} %shard_map.82.lhs, f32[512,128]{1,0:T(8,128)S(1)} %broadcast_in_dim.30.row_energy, f32[2,1024]{1,0:T(2,128)S(1)} %broadcast_subtract_fusion.col_energy, ...), custom_call_target="tpu_custom_call" | custom-call | tf_op jit(solution)/shard_map/pallas_call | solution.py:142
  (22 shorter events, 0.4 us)
Async XLA Ops:
  6.5 51.5 %copy-start.2 = (s32[4]{0:T(128)S(1)}, s32[4]{0:T(128)}, u32[]{:S(2)}) copy-start(s32[4]{0:T(128)} %param.12) | copy-start | bytes 52
  6.5 51.5 %copy-start.1 = (s32[16]{0:T(128)S(1)}, s32[16]{0:T(128)}, u32[]{:S(2)}) copy-start(s32[16]{0:T(128)} %param.11) | copy-start | bytes 196
  6.5 52.5 %copy-start = (s32[8,2,8,8]{3,2,1,0:T(8,128)S(1)}, s32[8,2,8,8]{3,2,1,0:T(8,128)}, u32[]{:S(2)}) copy-start(s32[8,2,8,8]{3,2,1,0:T(8,128)} %param.10) | copy-start | bytes 12292
  6.5 67.1 %all-gather.2.cloned.1.call-start = ((), (), s32[]{:S(2)}) async-start(), calls=%async_computation.3 | async-start | bytes 8912896 | tf_op jit(solution)/shard_map/all_gather | solution.py:185
  28.0 22.8 %all-to-all-start.1 = ((bf16[8,8,32,128]{3,2,1,0:T(8,128)(2,1)}), bf16[8,8,32,128]{3,2,1,0:T(8,128)(2,1)S(1)}, u32[]{:S(2)}, u32[]{:S(2)}) async-start(bf16[8,8,32,128]{3,2,1,0:T(8,128)(2,1)} %broadcast_in_dim.26), calls=%async_computation.1 | async-start | bytes 1048576 | tf_op jit(solution)/shard_map/all_to_all | solution.py:19
  52.1 17.5 %all-to-all-start.2 = ((bf16[4,4,8,32,128]{4,3,2,1,0:T(8,128)(2,1)}), bf16[4,4,8,32,128]{4,3,2,1,0:T(8,128)(2,1)S(1)}, u32[]{:S(2)}, u32[]{:S(2)}) async-start(bf16[4,4,8,32,128]{4,3,2,1,0:T(8,128)(2,1)} %broadcast_in_dim.29), calls=%async_computation.2 | async-start | bytes 2097152 | tf_op jit(solution)/shard_map/all_to_all | solution.py:19
Sparse Core Ops, SparseCore 0:
  9.5 64.1 all-gather.1
where the time goes:
time: 86.9 us; the launch traced here: 86.4 us
  between operations  20.6 us (24%)
  starting transfers between devices  17.3 us (20%)
  blocking collectives  17.1 us (20%)
  waiting for transfers between devices  12.7 us (15%)
  local copies, waits for them, and re-layouts  9.57 us (11%)
  Pallas kernels  7.41 us (9%)
  other arithmetic  1.73 us (2%)
    all_to_all x2, starting transfers between devices, gather_by_exchange(): lax.all_to_all(copies, 'summa', 0, 0, axis_index_groups=groups, tiled=True)  17.3 us
    all_to_all x1, blocking collectives, body(): blocks = lax.all_to_all(blocks, 'perm', 0, 0, tiled=True)  17.1 us
    all_to_all x2, waiting for transfers between devices, gather_by_exchange(): lax.all_to_all(copies, 'summa', 0, 0, axis_index_groups=groups, tiled=True)  10.4 us
    pallas_call x1, Pallas kernels, contract(): pl.pallas_call(contract_kernel, out_shape=jax.ShapeDtypeStruct((row_count...  5.91 us
    all_gather x1, waiting for transfers between devices, body(): slots = lax.all_gather(by_part.reshape(-1, LANES), 'perm', axis=0)  2.34 us
    broadcast_in_dim x2, local copies, waits for them, and re-layouts, gather_by_exchange(): copies = jnp.broadcast_to(value[None], (count, *value.shape))  2.06 us
    transpose x1, local copies, waits for them, and re-layouts, body(): jnp.transpose(as_given.reshape(width, parts, col_local, LANES), (2, 1, 0,...  2.03 us
  transfers between devices with their start and end apart: 3, of which 3 were waited for; matrix products, arithmetic and copies ran while one was open for 11% of the time, Pallas kernels for 2%

commit v1 on v0

--- a/solution.py
+++ b/solution.py
@@ -77,7 +77,8 @@
     beside = MXU // LANES
     some = MXU // (parts * cols)
     order = together(parts, cols, some)
-    steps = [(j, part) for j in range(cols) for part in range(0, parts, beside)]
+    wide = parts // 2
+    steps = [(j, part) for j in range(cols) for part in range(0, parts, wide)]
 
     def product(j, part):
         if part == 0:
@@ -85,14 +86,14 @@
                 fetch.wait()
         rhs = [
             panels[j, :, pl.ds(one * width, width), :].reshape(depth, LANES)
-            for one in range(part, part + beside)
+            for one in range(part, part + wide)
         ]
         return jnp.dot(
             lhs[...], jnp.concatenate(rhs, axis=1), preferred_element_type=jnp.float32
         )
 
     def finish(term, j, part):
-        for one in range(beside):
+        for one in range(wide):
             gap = row_energy[...] + col_energy[pl.ds(j, 1), pl.ds((part + one) * LANES, LANES)]
             guess = pl.reciprocal(gap, approx=True)
             value = term[:, one * LANES : (one + 1) * LANES] * (guess * (2.0 - gap * guess))

time: 86.9 us -> 87 us (level)
  no operation moved by 1% of the time
where the time goes in v1:
time: 87 us; the launch traced here: 86.5 us
  between operations  20.6 us (24%)
  starting transfers between devices  17.3 us (20%)
  blocking collectives  17.1 us (20%)
  waiting for transfers between devices  12.7 us (15%)
  local copies, waits for them, and re-layouts  9.57 us (11%)
  Pallas kernels  7.47 us (9%)
  other arithmetic  1.73 us (2%)
    all_to_all x2, starting transfers between devices, gather_by_exchange(): lax.all_to_all(copies, 'summa', 0, 0, axis_index_groups=groups, tiled=True)  17.3 us
    all_to_all x1, blocking collectives, body(): blocks = lax.all_to_all(blocks, 'perm', 0, 0, tiled=True)  17.1 us
    all_to_all x2, waiting for transfers between devices, gather_by_exchange(): lax.all_to_all(copies, 'summa', 0, 0, axis_index_groups=groups, tiled=True)  10.4 us
    pallas_call x1, Pallas kernels, contract(): pl.pallas_call(contract_kernel, out_shape=jax.ShapeDtypeStruct((row_count...  5.97 us
    all_gather x1, waiting for transfers between devices, body(): slots = lax.all_gather(by_part.reshape(-1, LANES), 'perm', axis=0)  2.34 us
    broadcast_in_dim x2, local copies, waits for them, and re-layouts, gather_by_exchange(): copies = jnp.broadcast_to(value[None], (count, *value.shape))  2.06 us
    transpose x1, local copies, waits for them, and re-layouts, body(): jnp.transpose(as_given.reshape(width, parts, col_local, LANES), (2, 1, 0,...  2.03 us
  transfers between devices with their start and end apart: 3, of which 3 were waited for; matrix products, arithmetic and copies ran while one was open for 11% of the time, Pallas kernels for 2%

profile of v1, /device:TPU:1, one launch (start us, length us, event | category | flops | bytes accessed | tf_op | source)
XLA Modules:
  0.0 86.5 jit_solution(1269020974386432543)
XLA Ops:
  6.5 2.0 %copy.42 = bf16[2,8,128,128]{3,2,1,0:T(8,128)(2,1)} copy(bf16[2,8,128,128]{3,0,1,2:T(2,128)(2,1)} %bitcast.39) | data formatting | bytes 1048576 | tf_op jit(solution)/shard_map/transpose | solution.py:185
  8.6 1.0 %reshape.80 = bf16[32,16,64]{2,1,0:T(8,128)(2,1)S(1)} reshape(bf16[32,1024]{1,0:T(8,128)(2,1)} %bitcast.42) | data formatting | bytes 131072 | tf_op jit(solution)/shard_map/reshape | solution.py:188
  9.7 0.1 reshape.106
  9.8 17.1 %all_to_all.15 = bf16[16,2,1024]{2,1,0:T(2,128)(2,1)S(1)} all-to-all(bf16[16,2,1024]{2,1,0:T(2,128)(2,1)S(1)} %reshape.106), channel_id=1, replica_groups=mesh['perm'=16,'summa'=32] {'perm'}, dimensions={0} | all-to-all | bytes 131072 | tf_op jit(solution)/shard_map/all_to_all | solution.py:189
  26.9 0.1 reshape.107
  27.1 0.1 pad_maximum_fusion.1
  27.2 0.9 %broadcast_in_dim.26 = bf16[8,8,32,128]{3,2,1,0:T(8,128)(2,1)} broadcast(bf16[8,32,128]{2,1,0:T(8,128)(2,1)S(1)} %pad_maximum_fusion.1), dimensions={1,2,3} | broadcast | bytes 589824 | tf_op jit(solution)/shard_map/broadcast_in_dim | solution.py:18
  28.0 11.3 %all-to-all-start.1 = ((bf16[8,8,32,128]{3,2,1,0:T(8,128)(2,1)}), bf16[8,8,32,128]{3,2,1,0:T(8,128)(2,1)S(1)}, u32[]{:S(2)}, u32[]{:S(2)}) async-start(bf16[8,8,32,128]{3,2,1,0:T(8,128)(2,1)} %broadcast_in_dim.26), calls=%async_computation.1 | async-start | bytes 1048576 | tf_op jit(solution)/shard_map/all_to_all | solution.py:19
  39.4 0.7 or_and_fusion
  40.0 0.6 fusion
  47.7 0.8 dynamic_slice.24
  48.4 0.1 sub.42
  48.5 0.1 sub.43
  48.6 0.7 sub.44
  49.3 0.1 sub.45
  49.4 0.8 broadcast_subtract_fusion.col_energy
  50.1 0.7 all-to-all-done.1
  50.9 1.2 %broadcast_in_dim.29 = bf16[4,4,8,32,128]{4,3,2,1,0:T(8,128)(2,1)} broadcast(bf16[4,8,32,128]{3,2,1,0:T(8,128)(2,1)S(1)} %pad_maximum_fusion), dimensions={1,2,3,4} | broadcast | bytes 1310720 | tf_op jit(solution)/shard_map/broadcast_in_dim | solution.py:18
  52.1 6.0 %all-to-all-start.2 = ((bf16[4,4,8,32,128]{4,3,2,1,0:T(8,128)(2,1)}), bf16[4,4,8,32,128]{4,3,2,1,0:T(8,128)(2,1)S(1)}, u32[]{:S(2)}, u32[]{:S(2)}) async-start(bf16[4,4,8,32,128]{4,3,2,1,0:T(8,128)(2,1)} %broadcast_in_dim.29), calls=%async_computation.2 | async-start | bytes 2097152 | tf_op jit(solution)/shard_map/all_to_all | solution.py:19
  58.1 0.1 reshape.82
  58.1 0.1 copy.39
  58.2 0.6 gather_fusion.1
  58.9 0.1 copy.40
  59.0 0.1 select_n.59
  59.1 0.1 copy.37
  59.2 0.6 gather_fusion
  59.7 0.1 convert_bitcast_fusion
  59.8 9.7 %all-to-all-done.2.tiles = bf16[4,4,8,32,128]{4,3,2,1,0:T(8,128)(2,1)S(1)} async-done(((bf16[4,4,8,32,128]{4,3,2,1,0:T(8,128)(2,1)}), bf16[4,4,8,32,128]{4,3,2,1,0:T(8,128)(2,1)S(1)}, u32[]{:S(2)}, u32[]{:S(2)}) %all-to-all-start.2) | async-done | bytes 1048608 | tf_op jit(solution)/shard_map/all_to_all | solution.py:19
  69.5 0.1 broadcast_in_dim.30.row_energy
  69.8 1.5 %shard_map.82.lhs = bf16[512,1024]{1,0:T(8,128)(2,1)S(1)} custom-call(f32[8,8,128]{2,1,0:T(8,128)S(1)} %broadcast_in_dim.56.keep, bf16[4,4,8,32,128]{4,3,2,1,0:T(8,128)(2,1)S(1)} %all-to-all-done.2.tiles), custom_call_target="tpu_custom_call" | custom-call | tf_op jit(solution)/shard_map/pallas_call | solution.py:50
  71.3 2.3 %all-gather.2.cloned.1.call-done.slots = bf16[16,2048,128]{2,1,0:T(8,128)(2,1)} async-done(((bf16[1,2048,128]{2,1,0:T(8,128)(2,1)}), bf16[16,2048,128]{2,1,0:T(8,128)(2,1)}) %all-gather.2.cloned.1.call-update) | async-done | bytes 8388624 | tf_op jit(solution)/shard_map/all_gather | solution.py:186
  73.6 6.0 %shard_map.83 = bf16[8192,128]{1,0:T(8,128)(2,1)} custom-call(s32[8,128]{1,0:T(8,128)S(1)} %broadcast_in_dim.58.chosen, bf16[512,1024]{1,0:T(8,128)(2,1)S(1)} %shard_map.82.lhs, f32[512,128]{1,0:T(8,128)S(1)} %broadcast_in_dim.30.row_energy, f32[2,1024]{1,0:T(2,128)S(1)} %broadcast_subtract_fusion.col_energy, ...), custom_call_target="tpu_custom_call" | custom-call | tf_op jit(solution)/shard_map/pallas_call | solution.py:143
  (22 shorter events, 0.4 us)
Async XLA Ops:
  6.5 51.5 %copy-start.2 = (s32[4]{0:T(128)S(1)}, s32[4]{0:T(128)}, u32[]{:S(2)}) copy-start(s32[4]{0:T(128)} %param.12) | copy-start | bytes 52
  6.5 51.5 %copy-start.1 = (s32[16]{0:T(128)S(1)}, s32[16]{0:T(128)}, u32[]{:S(2)}) copy-start(s32[16]{0:T(128)} %param.11) | copy-start | bytes 196
  6.5 52.5 %copy-start = (s32[8,2,8,8]{3,2,1,0:T(8,128)S(1)}, s32[8,2,8,8]{3,2,1,0:T(8,128)}, u32[]{:S(2)}) copy-start(s32[8,2,8,8]{3,2,1,0:T(8,128)} %param.10) | copy-start | bytes 12292
  6.5 67.1 %all-gather.2.cloned.1.call-start = ((), (), s32[]{:S(2)}) async-start(), calls=%async_computation.3 | async-start | bytes 8912896 | tf_op jit(solution)/shard_map/all_gather | solution.py:186
  28.0 22.8 %all-to-all-start.1 = ((bf16[8,8,32,128]{3,2,1,0:T(8,128)(2,1)}), bf16[8,8,32,128]{3,2,1,0:T(8,128)(2,1)S(1)}, u32[]{:S(2)}, u32[]{:S(2)}) async-start(bf16[8,8,32,128]{3,2,1,0:T(8,128)(2,1)} %broadcast_in_dim.26), calls=%async_computation.1 | async-start | bytes 1048576 | tf_op jit(solution)/shard_map/all_to_all | solution.py:19
  52.1 17.5 %all-to-all-start.2 = ((bf16[4,4,8,32,128]{4,3,2,1,0:T(8,128)(2,1)}), bf16[4,4,8,32,128]{4,3,2,1,0:T(8,128)(2,1)S(1)}, u32[]{:S(2)}, u32[]{:S(2)}) async-start(bf16[4,4,8,32,128]{4,3,2,1,0:T(8,128)(2,1)} %broadcast_in_dim.29), calls=%async_computation.2 | async-start | bytes 2097152 | tf_op jit(solution)/shard_map/all_to_all | solution.py:19
Sparse Core Ops, SparseCore 0:
  9.5 64.1 all-gather.1

commit v2 on v1

--- a/solution.py
+++ b/solution.py
@@ -77,37 +77,38 @@
     beside = MXU // LANES
     some = MXU // (parts * cols)
     order = together(parts, cols, some)
-    wide = parts // 2
-    steps = [(j, part) for j in range(cols) for part in range(0, parts, wide)]
-
-    def product(j, part):
-        if part == 0:
-            for fetch in fetches[j * count : (j + 1) * count]:
-                fetch.wait()
+    stores = []
+
+    def product(j, part, wide, low, size):
         rhs = [
             panels[j, :, pl.ds(one * width, width), :].reshape(depth, LANES)
             for one in range(part, part + wide)
         ]
         return jnp.dot(
-            lhs[...], jnp.concatenate(rhs, axis=1), preferred_element_type=jnp.float32
+            lhs[pl.ds(low, size), :],
+            jnp.concatenate(rhs, axis=1),
+            preferred_element_type=jnp.float32,
         )
 
-    def finish(term, j, part):
+    def finish(term, j, part, wide, low, size):
         for one in range(wide):
-            gap = row_energy[...] + col_energy[pl.ds(j, 1), pl.ds((part + one) * LANES, LANES)]
+            gap = row_energy[pl.ds(low, size), :]
+            gap = gap + col_energy[pl.ds(j, 1), pl.ds((part + one) * LANES, LANES)]
             guess = pl.reciprocal(gap, approx=True)
             value = term[:, one * LANES : (one + 1) * LANES] * (guess * (2.0 - gap * guess))
-            values[part + one, j] = value.astype(out.dtype)
-
-    term = product(*steps[0])
-    for now, later in zip(steps, steps[1:] + [None]):
-        ahead = product(*later) if later else None
-        finish(term, *now)
-        term = ahead
-    stores = []
+            values[part + one, j, pl.ds(low, size), :] = value.astype(out.dtype)
+
+    def run(steps):
+        term = product(*steps[0])
+        for now, later in zip(steps, steps[1:] + [None]):
+            ahead = product(*later) if later else None
+            finish(term, *now)
+            term = ahead
+
     rows_of = parts * cols
     span = row_count // left.shape[0]
-    for m in range(0, row_count, some * beside):
+
+    def join(m):
         apart = [
             jnp.concatenate(
                 [
@@ -128,6 +129,27 @@
             store = pltpu.make_async_copy(done.at[rows], out.at[rows], left.at[m // span])
             store.start()
             stores.append(store)
+
+    for j in range(cols):
+        for fetch in fetches[j * count : (j + 1) * count]:
+            fetch.wait()
+        if j < cols - 1:
+            run([(j, part, parts // 2, 0, row_count) for part in range(0, parts, parts // 2)])
+    half = row_count // 2
+    first, second = [
+        [(cols - 1, part, beside, low, half) for part in range(0, parts, beside)]
+        for low in (0, half)
+    ]
+    run(first)
+    groups = list(range(0, half, some * beside))
+    each = len(groups) // len(second)
+    for n, step in enumerate(second):
+        term = product(*step)
+        for m in groups[n * each : (n + 1) * each]:
+            join(m)
+        finish(term, *step)
+    for m in range(half, row_count, some * beside):
+        join(m)
     for store in stores:
         store.wait()
 

time: 87 us -> 87 us (level)
  no operation moved by 1% of the time
where the time goes in v2:
time: 87 us; the launch traced here: 86.5 us
  between operations  20.6 us (24%)
  starting transfers between devices  17.3 us (20%)
  blocking collectives  17.1 us (20%)
  waiting for transfers between devices  12.7 us (15%)
  local copies, waits for them, and re-layouts  9.57 us (11%)
  Pallas kernels  7.46 us (9%)
  other arithmetic  1.73 us (2%)
    all_to_all x2, starting transfers between devices, gather_by_exchange(): lax.all_to_all(copies, 'summa', 0, 0, axis_index_groups=groups, tiled=True)  17.3 us
    all_to_all x1, blocking collectives, body(): blocks = lax.all_to_all(blocks, 'perm', 0, 0, tiled=True)  17.1 us
    all_to_all x2, waiting for transfers between devices, gather_by_exchange(): lax.all_to_all(copies, 'summa', 0, 0, axis_index_groups=groups, tiled=True)  10.4 us
    pallas_call x1, Pallas kernels, contract(): pl.pallas_call(contract_kernel, out_shape=jax.ShapeDtypeStruct((row_count...  5.96 us
    all_gather x1, waiting for transfers between devices, body(): slots = lax.all_gather(by_part.reshape(-1, LANES), 'perm', axis=0)  2.34 us
    broadcast_in_dim x2, local copies, waits for them, and re-layouts, gather_by_exchange(): copies = jnp.broadcast_to(value[None], (count, *value.shape))  2.06 us
    transpose x1, local copies, waits for them, and re-layouts, body(): jnp.transpose(as_given.reshape(width, parts, col_local, LANES), (2, 1, 0,...  2.03 us
  transfers between devices with their start and end apart: 3, of which 3 were waited for; matrix products, arithmetic and copies ran while one was open for 11% of the time, Pallas kernels for 2%

profile of v2, /device:TPU:1, one launch (start us, length us, event | category | flops | bytes accessed | tf_op | source)
XLA Modules:
  0.0 86.5 jit_solution(1570107595848371607)
XLA Ops:
  6.5 2.0 %copy.42 = bf16[2,8,128,128]{3,2,1,0:T(8,128)(2,1)} copy(bf16[2,8,128,128]{3,0,1,2:T(2,128)(2,1)} %bitcast.39) | data formatting | bytes 1048576 | tf_op jit(solution)/shard_map/transpose | solution.py:207
  8.6 1.0 %reshape.80 = bf16[32,16,64]{2,1,0:T(8,128)(2,1)S(1)} reshape(bf16[32,1024]{1,0:T(8,128)(2,1)} %bitcast.42) | data formatting | bytes 131072 | tf_op jit(solution)/shard_map/reshape | solution.py:210
  9.7 0.1 reshape.106
  9.8 17.1 %all_to_all.15 = bf16[16,2,1024]{2,1,0:T(2,128)(2,1)S(1)} all-to-all(bf16[16,2,1024]{2,1,0:T(2,128)(2,1)S(1)} %reshape.106), channel_id=1, replica_groups=mesh['perm'=16,'summa'=32] {'perm'}, dimensions={0} | all-to-all | bytes 131072 | tf_op jit(solution)/shard_map/all_to_all | solution.py:211
  26.9 0.1 reshape.107
  27.1 0.1 pad_maximum_fusion.1
  27.2 0.9 %broadcast_in_dim.26 = bf16[8,8,32,128]{3,2,1,0:T(8,128)(2,1)} broadcast(bf16[8,32,128]{2,1,0:T(8,128)(2,1)S(1)} %pad_maximum_fusion.1), dimensions={1,2,3} | broadcast | bytes 589824 | tf_op jit(solution)/shard_map/broadcast_in_dim | solution.py:18
  28.0 11.3 %all-to-all-start.1 = ((bf16[8,8,32,128]{3,2,1,0:T(8,128)(2,1)}), bf16[8,8,32,128]{3,2,1,0:T(8,128)(2,1)S(1)}, u32[]{:S(2)}, u32[]{:S(2)}) async-start(bf16[8,8,32,128]{3,2,1,0:T(8,128)(2,1)} %broadcast_in_dim.26), calls=%async_computation.1 | async-start | bytes 1048576 | tf_op jit(solution)/shard_map/all_to_all | solution.py:19
  39.4 0.7 or_and_fusion
  40.0 0.6 fusion
  47.7 0.8 dynamic_slice.24
  48.4 0.1 sub.42
  48.5 0.1 sub.43
  48.6 0.7 sub.44
  49.3 0.1 sub.45
  49.4 0.8 broadcast_subtract_fusion.col_energy
  50.1 0.7 all-to-all-done.1
  50.9 1.2 %broadcast_in_dim.29 = bf16[4,4,8,32,128]{4,3,2,1,0:T(8,128)(2,1)} broadcast(bf16[4,8,32,128]{3,2,1,0:T(8,128)(2,1)S(1)} %pad_maximum_fusion), dimensions={1,2,3,4} | broadcast | bytes 1310720 | tf_op jit(solution)/shard_map/broadcast_in_dim | solution.py:18
  52.1 6.0 %all-to-all-start.2 = ((bf16[4,4,8,32,128]{4,3,2,1,0:T(8,128)(2,1)}), bf16[4,4,8,32,128]{4,3,2,1,0:T(8,128)(2,1)S(1)}, u32[]{:S(2)}, u32[]{:S(2)}) async-start(bf16[4,4,8,32,128]{4,3,2,1,0:T(8,128)(2,1)} %broadcast_in_dim.29), calls=%async_computation.2 | async-start | bytes 2097152 | tf_op jit(solution)/shard_map/all_to_all | solution.py:19
  58.1 0.1 reshape.82
  58.1 0.1 copy.39
  58.2 0.6 gather_fusion.1
  58.9 0.1 copy.40
  59.0 0.1 select_n.59
  59.1 0.1 copy.37
  59.2 0.6 gather_fusion
  59.7 0.1 convert_bitcast_fusion
  59.8 9.7 %all-to-all-done.2.tiles = bf16[4,4,8,32,128]{4,3,2,1,0:T(8,128)(2,1)S(1)} async-done(((bf16[4,4,8,32,128]{4,3,2,1,0:T(8,128)(2,1)}), bf16[4,4,8,32,128]{4,3,2,1,0:T(8,128)(2,1)S(1)}, u32[]{:S(2)}, u32[]{:S(2)}) %all-to-all-start.2) | async-done | bytes 1048608 | tf_op jit(solution)/shard_map/all_to_all | solution.py:19
  69.5 0.1 broadcast_in_dim.30.row_energy
  69.8 1.5 %shard_map.82.lhs = bf16[512,1024]{1,0:T(8,128)(2,1)S(1)} custom-call(f32[8,8,128]{2,1,0:T(8,128)S(1)} %broadcast_in_dim.56.keep, bf16[4,4,8,32,128]{4,3,2,1,0:T(8,128)(2,1)S(1)} %all-to-all-done.2.tiles), custom_call_target="tpu_custom_call" | custom-call | tf_op jit(solution)/shard_map/pallas_call | solution.py:50
  71.3 2.3 %all-gather.2.cloned.1.call-done.slots = bf16[16,2048,128]{2,1,0:T(8,128)(2,1)} async-done(((bf16[1,2048,128]{2,1,0:T(8,128)(2,1)}), bf16[16,2048,128]{2,1,0:T(8,128)(2,1)}) %all-gather.2.cloned.1.call-update) | async-done | bytes 8388624 | tf_op jit(solution)/shard_map/all_gather | solution.py:208
  73.6 6.0 %shard_map.83 = bf16[8192,128]{1,0:T(8,128)(2,1)} custom-call(s32[8,128]{1,0:T(8,128)S(1)} %broadcast_in_dim.58.chosen, bf16[512,1024]{1,0:T(8,128)(2,1)S(1)} %shard_map.82.lhs, f32[512,128]{1,0:T(8,128)S(1)} %broadcast_in_dim.30.row_energy, f32[2,1024]{1,0:T(2,128)S(1)} %broadcast_subtract_fusion.col_energy, ...), custom_call_target="tpu_custom_call" | custom-call | tf_op jit(solution)/shard_map/pallas_call | solution.py:165
  (22 shorter events, 0.4 us)
Async XLA Ops:
  6.5 51.5 %copy-start.2 = (s32[4]{0:T(128)S(1)}, s32[4]{0:T(128)}, u32[]{:S(2)}) copy-start(s32[4]{0:T(128)} %param.12) | copy-start | bytes 52
  6.5 51.5 %copy-start.1 = (s32[16]{0:T(128)S(1)}, s32[16]{0:T(128)}, u32[]{:S(2)}) copy-start(s32[16]{0:T(128)} %param.11) | copy-start | bytes 196
  6.5 52.5 %copy-start = (s32[8,2,8,8]{3,2,1,0:T(8,128)S(1)}, s32[8,2,8,8]{3,2,1,0:T(8,128)}, u32[]{:S(2)}) copy-start(s32[8,2,8,8]{3,2,1,0:T(8,128)} %param.10) | copy-start | bytes 12292
  6.5 67.1 %all-gather.2.cloned.1.call-start = ((), (), s32[]{:S(2)}) async-start(), calls=%async_computation.3 | async-start | bytes 8912896 | tf_op jit(solution)/shard_map/all_gather | solution.py:208
  28.0 22.8 %all-to-all-start.1 = ((bf16[8,8,32,128]{3,2,1,0:T(8,128)(2,1)}), bf16[8,8,32,128]{3,2,1,0:T(8,128)(2,1)S(1)}, u32[]{:S(2)}, u32[]{:S(2)}) async-start(bf16[8,8,32,128]{3,2,1,0:T(8,128)(2,1)} %broadcast_in_dim.26), calls=%async_computation.1 | async-start | bytes 1048576 | tf_op jit(solution)/shard_map/all_to_all | solution.py:19
  52.1 17.5 %all-to-all-start.2 = ((bf16[4,4,8,32,128]{4,3,2,1,0:T(8,128)(2,1)}), bf16[4,4,8,32,128]{4,3,2,1,0:T(8,128)(2,1)S(1)}, u32[]{:S(2)}, u32[]{:S(2)}) async-start(bf16[4,4,8,32,128]{4,3,2,1,0:T(8,128)(2,1)} %broadcast_in_dim.29), calls=%async_computation.2 | async-start | bytes 2097152 | tf_op jit(solution)/shard_map/all_to_all | solution.py:19
Sparse Core Ops, SparseCore 0:
  9.5 64.1 all-gather.1

commit v3 on v2

--- a/solution.py
+++ b/solution.py
@@ -72,8 +72,8 @@
             fetches.append(
                 pltpu.make_async_copy(slots.at[slot[m], rows], panels.at[j, m], came.at[j, m])
             )
-    for fetch in fetches:
-        fetch.start()
+    for n, fetch in enumerate(fetches):
+        fetch.start(priority=n & 1)
     beside = MXU // LANES
     some = MXU // (parts * cols)
     order = together(parts, cols, some)

time: 87 us -> 87.3 us (level)
  no operation moved by 1% of the time
where the time goes in v3:
time: 87.3 us; the launch traced here: 86.8 us
  between operations  20.6 us (24%)
  starting transfers between devices  17.3 us (20%)
  blocking collectives  17.1 us (20%)
  waiting for transfers between devices  12.7 us (15%)
  local copies, waits for them, and re-layouts  9.57 us (11%)
  Pallas kernels  7.77 us (9%)
  other arithmetic  1.73 us (2%)
    all_to_all x2, starting transfers between devices, gather_by_exchange(): lax.all_to_all(copies, 'summa', 0, 0, axis_index_groups=groups, tiled=True)  17.3 us
    all_to_all x1, blocking collectives, body(): blocks = lax.all_to_all(blocks, 'perm', 0, 0, tiled=True)  17.1 us
    all_to_all x2, waiting for transfers between devices, gather_by_exchange(): lax.all_to_all(copies, 'summa', 0, 0, axis_index_groups=groups, tiled=True)  10.4 us
    pallas_call x1, Pallas kernels, contract(): pl.pallas_call(contract_kernel, out_shape=jax.ShapeDtypeStruct((row_count...  6.27 us
    all_gather x1, waiting for transfers between devices, body(): slots = lax.all_gather(by_part.reshape(-1, LANES), 'perm', axis=0)  2.34 us
    broadcast_in_dim x2, local copies, waits for them, and re-layouts, gather_by_exchange(): copies = jnp.broadcast_to(value[None], (count, *value.shape))  2.06 us
    transpose x1, local copies, waits for them, and re-layouts, body(): jnp.transpose(as_given.reshape(width, parts, col_local, LANES), (2, 1, 0,...  2.03 us
  transfers between devices with their start and end apart: 3, of which 3 were waited for; matrix products, arithmetic and copies ran while one was open for 11% of the time, Pallas kernels for 2%

profile of v3, /device:TPU:1, one launch (start us, length us, event | category | flops | bytes accessed | tf_op | source)
XLA Modules:
  0.0 86.8 jit_solution(13747028292225915518)
XLA Ops:
  6.5 2.0 %copy.42 = bf16[2,8,128,128]{3,2,1,0:T(8,128)(2,1)} copy(bf16[2,8,128,128]{3,0,1,2:T(2,128)(2,1)} %bitcast.39) | data formatting | bytes 1048576 | tf_op jit(solution)/shard_map/transpose | solution.py:207
  8.6 1.0 %reshape.80 = bf16[32,16,64]{2,1,0:T(8,128)(2,1)S(1)} reshape(bf16[32,1024]{1,0:T(8,128)(2,1)} %bitcast.42) | data formatting | bytes 131072 | tf_op jit(solution)/shard_map/reshape | solution.py:210
  9.7 0.1 reshape.106
  9.8 17.1 %all_to_all.15 = bf16[16,2,1024]{2,1,0:T(2,128)(2,1)S(1)} all-to-all(bf16[16,2,1024]{2,1,0:T(2,128)(2,1)S(1)} %reshape.106), channel_id=1, replica_groups=mesh['perm'=16,'summa'=32] {'perm'}, dimensions={0} | all-to-all | bytes 131072 | tf_op jit(solution)/shard_map/all_to_all | solution.py:211
  26.9 0.1 reshape.107
  27.1 0.1 pad_maximum_fusion.1
  27.2 0.9 %broadcast_in_dim.26 = bf16[8,8,32,128]{3,2,1,0:T(8,128)(2,1)} broadcast(bf16[8,32,128]{2,1,0:T(8,128)(2,1)S(1)} %pad_maximum_fusion.1), dimensions={1,2,3} | broadcast | bytes 589824 | tf_op jit(solution)/shard_map/broadcast_in_dim | solution.py:18
  28.0 11.3 %all-to-all-start.1 = ((bf16[8,8,32,128]{3,2,1,0:T(8,128)(2,1)}), bf16[8,8,32,128]{3,2,1,0:T(8,128)(2,1)S(1)}, u32[]{:S(2)}, u32[]{:S(2)}) async-start(bf16[8,8,32,128]{3,2,1,0:T(8,128)(2,1)} %broadcast_in_dim.26), calls=%async_computation.1 | async-start | bytes 1048576 | tf_op jit(solution)/shard_map/all_to_all | solution.py:19
  39.4 0.7 or_and_fusion
  40.0 0.6 fusion
  47.7 0.8 dynamic_slice.24
  48.4 0.1 sub.42
  48.5 0.1 sub.43
  48.6 0.7 sub.44
  49.3 0.1 sub.45
  49.4 0.8 broadcast_subtract_fusion.col_energy
  50.1 0.7 all-to-all-done.1
  50.9 1.2 %broadcast_in_dim.29 = bf16[4,4,8,32,128]{4,3,2,1,0:T(8,128)(2,1)} broadcast(bf16[4,8,32,128]{3,2,1,0:T(8,128)(2,1)S(1)} %pad_maximum_fusion), dimensions={1,2,3,4} | broadcast | bytes 1310720 | tf_op jit(solution)/shard_map/broadcast_in_dim | solution.py:18
  52.1 6.0 %all-to-all-start.2 = ((bf16[4,4,8,32,128]{4,3,2,1,0:T(8,128)(2,1)}), bf16[4,4,8,32,128]{4,3,2,1,0:T(8,128)(2,1)S(1)}, u32[]{:S(2)}, u32[]{:S(2)}) async-start(bf16[4,4,8,32,128]{4,3,2,1,0:T(8,128)(2,1)} %broadcast_in_dim.29), calls=%async_computation.2 | async-start | bytes 2097152 | tf_op jit(solution)/shard_map/all_to_all | solution.py:19
  58.1 0.1 reshape.82
  58.1 0.1 copy.39
  58.2 0.6 gather_fusion.1
  58.9 0.1 copy.40
  59.0 0.1 select_n.59
  59.1 0.1 copy.37
  59.2 0.6 gather_fusion
  59.7 0.1 convert_bitcast_fusion
  59.8 9.7 %all-to-all-done.2.tiles = bf16[4,4,8,32,128]{4,3,2,1,0:T(8,128)(2,1)S(1)} async-done(((bf16[4,4,8,32,128]{4,3,2,1,0:T(8,128)(2,1)}), bf16[4,4,8,32,128]{4,3,2,1,0:T(8,128)(2,1)S(1)}, u32[]{:S(2)}, u32[]{:S(2)}) %all-to-all-start.2) | async-done | bytes 1048608 | tf_op jit(solution)/shard_map/all_to_all | solution.py:19
  69.5 0.1 broadcast_in_dim.30.row_energy
  69.8 1.5 %shard_map.82.lhs = bf16[512,1024]{1,0:T(8,128)(2,1)S(1)} custom-call(f32[8,8,128]{2,1,0:T(8,128)S(1)} %broadcast_in_dim.56.keep, bf16[4,4,8,32,128]{4,3,2,1,0:T(8,128)(2,1)S(1)} %all-to-all-done.2.tiles), custom_call_target="tpu_custom_call" | custom-call | tf_op jit(solution)/shard_map/pallas_call | solution.py:50
  71.3 2.3 %all-gather.2.cloned.1.call-done.slots = bf16[16,2048,128]{2,1,0:T(8,128)(2,1)} async-done(((bf16[1,2048,128]{2,1,0:T(8,128)(2,1)}), bf16[16,2048,128]{2,1,0:T(8,128)(2,1)}) %all-gather.2.cloned.1.call-update) | async-done | bytes 8388624 | tf_op jit(solution)/shard_map/all_gather | solution.py:208
  73.6 6.3 %shard_map.83 = bf16[8192,128]{1,0:T(8,128)(2,1)} custom-call(s32[8,128]{1,0:T(8,128)S(1)} %broadcast_in_dim.58.chosen, bf16[512,1024]{1,0:T(8,128)(2,1)S(1)} %shard_map.82.lhs, f32[512,128]{1,0:T(8,128)S(1)} %broadcast_in_dim.30.row_energy, f32[2,1024]{1,0:T(2,128)S(1)} %broadcast_subtract_fusion.col_energy, ...), custom_call_target="tpu_custom_call" | custom-call | tf_op jit(solution)/shard_map/pallas_call | solution.py:165
  (22 shorter events, 0.4 us)
Async XLA Ops:
  6.5 51.5 %copy-start.2 = (s32[4]{0:T(128)S(1)}, s32[4]{0:T(128)}, u32[]{:S(2)}) copy-start(s32[4]{0:T(128)} %param.12) | copy-start | bytes 52
  6.5 51.5 %copy-start.1 = (s32[16]{0:T(128)S(1)}, s32[16]{0:T(128)}, u32[]{:S(2)}) copy-start(s32[16]{0:T(128)} %param.11) | copy-start | bytes 196
  6.5 52.5 %copy-start = (s32[8,2,8,8]{3,2,1,0:T(8,128)S(1)}, s32[8,2,8,8]{3,2,1,0:T(8,128)}, u32[]{:S(2)}) copy-start(s32[8,2,8,8]{3,2,1,0:T(8,128)} %param.10) | copy-start | bytes 12292
  6.5 67.1 %all-gather.2.cloned.1.call-start = ((), (), s32[]{:S(2)}) async-start(), calls=%async_computation.3 | async-start | bytes 8912896 | tf_op jit(solution)/shard_map/all_gather | solution.py:208
  28.0 22.8 %all-to-all-start.1 = ((bf16[8,8,32,128]{3,2,1,0:T(8,128)(2,1)}), bf16[8,8,32,128]{3,2,1,0:T(8,128)(2,1)S(1)}, u32[]{:S(2)}, u32[]{:S(2)}) async-start(bf16[8,8,32,128]{3,2,1,0:T(8,128)(2,1)} %broadcast_in_dim.26), calls=%async_computation.1 | async-start | bytes 1048576 | tf_op jit(solution)/shard_map/all_to_all | solution.py:19
  52.1 17.5 %all-to-all-start.2 = ((bf16[4,4,8,32,128]{4,3,2,1,0:T(8,128)(2,1)}), bf16[4,4,8,32,128]{4,3,2,1,0:T(8,128)(2,1)S(1)}, u32[]{:S(2)}, u32[]{:S(2)}) async-start(bf16[4,4,8,32,128]{4,3,2,1,0:T(8,128)(2,1)} %broadcast_in_dim.29), calls=%async_computation.2 | async-start | bytes 2097152 | tf_op jit(solution)/shard_map/all_to_all | solution.py:19
Sparse Core Ops, SparseCore 0:
  9.5 64.1 all-gather.1
